TPU v7x, 256 devices: a whole 4x4x8 slice. The times are simulated.
256 devices in a mesh: dp: 8 (over x, core), expert: 32 (over z, y).
Axes of the slice: x: 4, y: 4, z: 8, core: 2. Of those that a mesh axis runs over, the one named last changes fastest.
Arguments:
- tokens: bfloat16 [32768, 2048], P(('dp', 'expert')), may hold values from -6 to 6
- gates: float32 [32768, 8], P(('dp', 'expert')), may hold values from 0.02 to 0.4
- routes: int32 [32768, 8], P(('dp', 'expert')), may hold values from 0 to 31, all different within a row; in each aligned block of 128 rows (0 to 127, 128 to 255, ...) at most 40 rows name the same one
- cotangent: bfloat16 [32768, 2048], P(('dp', 'expert')), may hold values from -0.29882812 to 0.29882812
- w_in: bfloat16 [32, 2048, 768], P('expert'), may hold values from -0.125 to 0.125
- w_down: bfloat16 [32, 384, 2048], P('expert'), may hold values from -0.3125 to 0.3125
Outputs:
- mixed_out: bfloat16 [32768, 2048], P(('dp', 'expert'))
- grad_gates: float32 [32768, 8], P(('dp', 'expert'))
- grad_in: float32 [32, 2048, 768], P('expert', 'dp')
- grad_down: float32 [32, 384, 2048], P('expert', None, 'dp')
Inputs may be any that keep to these rules, and one draw needn't show every extreme that they name: `routes`: among the 128 rows of one device no expert is chosen by more than 40 rows, and on every device some expert is chosen by exactly 40 rows. A row names 8 different experts.
All inputs are finite; a program needn't handle non-finite values.
Results may differ from a plain program's by a relative error of at most 0.0058.
Values may be sent and summed in bfloat16 or wider, within the bound.
No kernel may reach another device: no remote copies, remote signals or barrier semaphores. Data moves between devices by JAX's collectives and lax.ppermute only.
A program may use at most 128 MiB of HBM per device.

v0:
```python
import jax
import jax.numpy as jnp
from jax import lax
from jax.sharding import PartitionSpec as P


def swiglu_rows(rows_in, w_in_e, w_down_e):
    hidden = w_down_e.shape[0]
    projected = jnp.dot(rows_in, w_in_e, preferred_element_type=jnp.float32)
    gate_pre = projected[:, :hidden]
    up_pre = projected[:, hidden:]
    sig_gate = jax.nn.sigmoid(gate_pre)
    hidden_act = (gate_pre * sig_gate * up_pre).astype(jnp.bfloat16)
    expert_out = jnp.dot(hidden_act, w_down_e, preferred_element_type=jnp.float32).astype(
        jnp.bfloat16
    )
    return (gate_pre, up_pre, sig_gate, hidden_act, expert_out)


def down_gradient(hidden_act, scaled_cot):
    return lax.dot_general(
        hidden_act, scaled_cot, (((0,), (0,)), ((), ())), preferred_element_type=jnp.float32
    )


def in_gradient(rows_in, gate_pre, up_pre, sig_gate, scaled_cot, w_down_e):
    grad_hidden = lax.dot_general(
        scaled_cot, w_down_e, (((1,), (1,)), ((), ())), preferred_element_type=jnp.float32
    )
    grad_up_pre = grad_hidden * gate_pre * sig_gate
    grad_gate_pre = grad_hidden * up_pre * sig_gate * (1.0 + gate_pre * (1.0 - sig_gate))
    grad_pre = jnp.concatenate([grad_gate_pre, grad_up_pre], 1).astype(jnp.bfloat16)
    return lax.dot_general(
        rows_in, grad_pre, (((0,), (0,)), ((), ())), preferred_element_type=jnp.float32
    )


def on_device(tokens, gates, routes, cotangent, w_in, w_down):
    tok_rows, model_width = tokens.shape
    top_count = routes.shape[1]
    owners = lax.axis_size("expert")
    capacity = min(tok_rows, tok_rows * top_count * 5 // (4 * owners))
    flat_routes = routes.reshape(-1)
    routed_rows = flat_routes.shape[0]
    onehot = (flat_routes[:, None] == jnp.arange(owners, dtype=jnp.int32)[None, :]).astype(
        jnp.int32
    )
    before = jnp.cumsum(onehot, 0) - onehot
    slot_index = jnp.sum(before * onehot, 1)
    target = flat_routes * capacity + slot_index
    source = (
        jnp.full((owners * capacity,), -1, jnp.int32)
        .at[target]
        .set(jnp.arange(routed_rows, dtype=jnp.int32))
    )
    filled = source >= 0
    picked = jnp.where(filled, source, 0)
    token_of = picked // top_count
    send_rows = jnp.where(filled[:, None], tokens[token_of], jnp.zeros((), jnp.bfloat16)).reshape(
        owners, capacity, model_width
    )
    w_in_e = w_in[0]
    w_down_e = w_down[0]
    arrived = lax.all_to_all(send_rows, "expert", split_axis=0, concat_axis=0, tiled=True)
    rows_in = arrived.reshape(-1, model_width)
    gate_pre, up_pre, sig_gate, hidden_act, expert_out = swiglu_rows(rows_in, w_in_e, w_down_e)
    returned = lax.all_to_all(
        expert_out.reshape(owners, capacity, model_width),
        "expert",
        split_axis=0,
        concat_axis=0,
        tiled=True,
    )
    row_out = (
        returned.reshape(-1, model_width)[target]
        .reshape(tok_rows, top_count, model_width)
        .astype(jnp.float32)
    )
    mixed_out = jnp.sum(gates[:, :, None] * row_out, 1).astype(jnp.bfloat16)
    grad_gates = jnp.sum(cotangent.astype(jnp.float32)[:, None, :] * row_out, 2)
    weight_rows = jnp.where(filled, gates.reshape(-1)[picked], jnp.zeros((), jnp.float32))
    scaled = (weight_rows[:, None] * cotangent[token_of].astype(jnp.float32)).astype(jnp.bfloat16)
    arrived_cot = lax.all_to_all(
        scaled.reshape(owners, capacity, model_width),
        "expert",
        split_axis=0,
        concat_axis=0,
        tiled=True,
    )
    scaled_cot = arrived_cot.reshape(-1, model_width)
    grad_down_part = down_gradient(hidden_act, scaled_cot)
    grad_in_part = in_gradient(rows_in, gate_pre, up_pre, sig_gate, scaled_cot, w_down_e)
    grad_in, grad_down = (
        lax.psum_scatter(grad_in_part, "dp", scatter_dimension=0, tiled=True),
        lax.psum_scatter(grad_down_part, "dp", scatter_dimension=1, tiled=True),
    )
    return (mixed_out, grad_gates, grad_in[None], grad_down[None])


def solution(mesh):
    placed = (
        P(("dp", "expert"), None),
        P(("dp", "expert"), None),
        P(("dp", "expert"), None),
        P(("dp", "expert"), None),
        P("expert", None, None),
        P("expert", None, None),
    )
    return jax.shard_map(
        on_device,
        mesh=mesh,
        in_specs=placed,
        out_specs=(
            P(("dp", "expert"), None),
            P(("dp", "expert"), None),
            P("expert", "dp", None),
            P("expert", None, "dp"),
        ),
        check_vma=False,
    )
```

profile of v0, /device:TPU:24, one launch (start us, length us, event | category | flops | bytes accessed | tf_op | source)
XLA Modules:
  0.0 479.7 jit_solution(2803671077812570359)
XLA Ops:
  7.2 0.0 copy-start
  7.2 0.8 broadcast_multiply_fusion
  8.0 0.9 copy.20
  8.9 0.1 eq.29
  9.0 0.1 eq.25
  9.1 0.1 copy.19
  9.2 0.1 mul.77
  9.3 9.0 %reduce-window.6 = s32[32,8,128]{2,1,0:T(8,128)S(1)} reduce-window(s32[32,8,128]{2,1,0:T(8,128)S(1)} %fusion.15, s32[]{:T(128)} %constant.14.clone.1), window={size=1x1x128 pad=0_0x0_0x127_0}, to_apply=%region_0.0 | reduce-window | flops 4161536 | bytes 262148 | tf_op jit(solution)/shard_map/reduce-window
  18.3 0.1 slice.24
  18.4 0.1 copy.22
  18.6 0.1 copy.23
  18.7 0.1 broadcast_add_fusion
  18.9 4.3 scatter_custom_fusion
  23.2 0.1 broadcast_in_dim.44
  23.3 11.9 %gather_fusion = bf16[1280,2048]{1,0:T(8,128)(2,1)} fusion(bf16[128,2048]{1,0:T(8,128)(2,1)} %param.6, s32[2048]{0:T(1024)S(1)} %pad_clamp_fusion.1), kind=kCustom, calls=%fused_computation | custom fusion | bytes 10490880 | tf_op jit(solution)/shard_map/gather | solution.py:59
  35.3 5.2 %broadcast_select_fusion = bf16[32,40,2048]{2,1,0:T(8,128)(2,1)} fusion(bf16[32,40,2048]{2,1,0:T(8,128)(2,1)} %bitcast.51, pred[32,40]{1,0:T(8,128)(4,1)S(1)} %broadcast_in_dim.44), kind=kLoop, calls=%fused_computation.12 | loop fusion | flops 2621440 | bytes 10487040 | tf_op jit(solution)/shard_map/jit(_where)/select_n | solution.py:59
  40.5 0.0 copy-start.3
  40.5 11.7 %all-to-all-start = ((bf16[32,40,2048]{2,1,0:T(8,128)(2,1)}), bf16[32,40,2048]{2,1,0:T(8,128)(2,1)}, u32[]{:S(2)}, u32[]{:S(2)}) async-start(bf16[32,40,2048]{2,1,0:T(8,128)(2,1)} %broadcast_select_fusion), calls=%async_computation | async-start | bytes 10485760 | tf_op jit(solution)/shard_map/all_to_all | solution.py:64
  52.2 0.0 copy-done.3
  52.2 0.1 copy.18
  52.3 0.1 reshape.106
  52.4 5.0 %gather_fusion.2 = f32[1280]{0:T(1024)S(1)} fusion(f32[1024]{0:T(1024)S(1)} %reshape.106, s32[2048]{0:T(1024)S(1)} %pad_clamp_fusion), kind=kCustom, calls=%fused_computation.2 | custom fusion | bytes 15360 | tf_op jit(solution)/shard_map/gather | solution.py:81
  57.4 0.1 mul.84
  57.5 11.9 %gather_fusion.3 = bf16[1280,2048]{1,0:T(8,128)(2,1)} fusion(bf16[128,2048]{1,0:T(8,128)(2,1)} %param.9, s32[2048]{0:T(1024)S(1)} %pad_clamp_fusion.1), kind=kCustom, calls=%fused_computation.3 | custom fusion | bytes 10490880 | tf_op jit(solution)/shard_map/gather | solution.py:82
  69.4 5.7 %fusion = bf16[32,40,2048]{2,1,0:T(8,128)(2,1)} fusion(bf16[32,40,2048]{2,1,0:T(8,128)(2,1)} %bitcast.50, f32[32,40]{1,0:T(8,128)S(1)} %mul.84), kind=kLoop, calls=%fused_computation.8 | loop fusion | flops 7864320 | bytes 10490880 | tf_op jit(solution)/shard_map/convert_element_type | solution.py:82
  75.1 95.9 %all-to-all-done = bf16[32,40,2048]{2,1,0:T(8,128)(2,1)} async-done(((bf16[32,40,2048]{2,1,0:T(8,128)(2,1)}), bf16[32,40,2048]{2,1,0:T(8,128)(2,1)}, u32[]{:S(2)}, u32[]{:S(2)}) %all-to-all-start) | async-done | bytes 5242912 | tf_op jit(solution)/shard_map/all_to_all | solution.py:64
  171.0 8.2 %all-to-all-start.2 = ((bf16[32,40,2048]{2,1,0:T(8,128)(2,1)}), bf16[32,40,2048]{2,1,0:T(8,128)(2,1)}, u32[]{:S(2)}, u32[]{:S(2)}) async-start(bf16[32,40,2048]{2,1,0:T(8,128)(2,1)} %fusion), calls=%async_computation.2 | async-start | bytes 10485760 | tf_op jit(solution)/shard_map/all_to_all | solution.py:83
  179.1 0.2 reduce-scatter.5.cloned.1.call-start
  179.4 0.0 copy-done
  179.4 8.7 %fusion.3 = f32[1280,768]{0,1:T(8,128)} fusion(bf16[1280,2048]{1,0:T(8,128)(2,1)} %bitcast.5, bf16[1,2048,768]{2,1,0:T(8,128)(2,1)S(1)} %copy-done), kind=kOutput, calls=%fused_computation.13 | convolution fusion | flops 4026531840 | bytes 12320768 | tf_op jit(solution)/shard_map/dot_general | solution.py:9
  188.0 109.2 %all-to-all-done.2 = bf16[32,40,2048]{2,1,0:T(8,128)(2,1)} async-done(((bf16[32,40,2048]{2,1,0:T(8,128)(2,1)}), bf16[32,40,2048]{2,1,0:T(8,128)(2,1)}, u32[]{:S(2)}, u32[]{:S(2)}) %all-to-all-start.2) | async-done | bytes 5242912 | tf_op jit(solution)/shard_map/all_to_all | solution.py:83
  297.3 7.9 %multiply_convert_fusion.1 = (bf16[1280,384]{0,1:T(8,128)(2,1)S(1)}, bf16[1280,384]{0,1:T(8,128)(2,1)}, bf16[1280,384]{0,1:T(8,128)(2,1)S(1)}) fusion(f32[1280,768]{0,1:T(8,128)} %fusion.3, bf16[1280,2048]{1,0:T(8,128)(2,1)} %bitcast.13, bf16[1,384,2048]{2,1,0:T(8,128)(2,1)} %param.11), kind=kOutput, calls=%fused_computation.20 | convolution fusion | flops 2021130240 | bytes 13697024 | tf_op jit(solution)/shard_map/dot_general | solution.py:27
  305.1 6.3 %fusion.21 = f32[384,2048]{1,0:T(8,128)} fusion(bf16[1280,384]{0,1:T(8,128)(2,1)S(1)} %get-tuple-element.14, bf16[1280,2048]{1,0:T(8,128)(2,1)} %bitcast.13), kind=kOutput, calls=%fused_computation.53 | convolution fusion | flops 2013265920 | bytes 9371648 | tf_op jit(solution)/shard_map/dot_general | solution.py:21
  311.5 0.0 reduce-scatter.5.cloned.1.call-update
  311.5 0.3 reduce-scatter.3.cloned.1.call-start
  311.8 9.8 %fusion.5 = f32[2048,768]{1,0:T(8,128)} fusion(bf16[1280,2048]{1,0:T(8,128)(2,1)} %bitcast.5, bf16[1280,384]{0,1:T(8,128)(2,1)} %get-tuple-element.13, bf16[1280,384]{0,1:T(8,128)(2,1)S(1)} %get-tuple-element.12), kind=kOutput, calls=%fused_computation.15 | convolution fusion | flops 4030464000 | bytes 13500416 | tf_op jit(solution)/shard_map/dot_general | solution.py:33
  321.6 0.0 copy-start.4
  321.6 0.0 reduce-scatter.3.cloned.1.call-update
  321.6 1.6 copy-done.4
  323.2 4.6 convolution_convert_fusion
  327.9 0.0 copy-start.2
  327.9 8.3 %all-to-all-start.1 = ((bf16[32,40,2048]{2,1,0:T(8,128)(2,1)}), bf16[32,40,2048]{2,1,0:T(8,128)(2,1)}, u32[]{:S(2)}, u32[]{:S(2)}) async-start(bf16[32,40,2048]{2,1,0:T(8,128)(2,1)} %bitcast.52), calls=%async_computation.1 | async-start | bytes 10485760 | tf_op jit(solution)/shard_map/all_to_all | solution.py:67
  336.1 0.0 copy-done.2
  336.1 1.1 convert_element_type.48
  337.2 117.0 %all-to-all-done.1 = bf16[32,40,2048]{2,1,0:T(8,128)(2,1)} async-done(((bf16[32,40,2048]{2,1,0:T(8,128)(2,1)}), bf16[32,40,2048]{2,1,0:T(8,128)(2,1)}, u32[]{:S(2)}, u32[]{:S(2)}) %all-to-all-start.1) | async-done | bytes 5242912 | tf_op jit(solution)/shard_map/all_to_all | solution.py:67
  454.2 0.0 copy-start.1
  454.2 12.1 %gather_fusion.1 = bf16[1024,2048]{1,0:T(8,128)(2,1)} fusion(bf16[1280,2048]{1,0:T(8,128)(2,1)} %bitcast.9, s32[1024]{0:T(1024)S(1)} %broadcast_clamp_fusion), kind=kCustom, calls=%fused_computation.1 | custom fusion | bytes 8392704 | tf_op jit(solution)/shard_map/gather | solution.py:75
  466.4 5.8 %fusion.2 = (f32[128,8]{1,0:T(8,128)S(1)}, bf16[128,2048]{1,0:T(8,128)(2,1)}) fusion(bf16[1024,2048]{1,0:T(8,128)(2,1)} %gather_fusion.1, f32[128,2048]{1,0:T(8,128)} %convert_element_type.48, f32[128,8]{1,0:T(8,128)S(1)} %copy.18), kind=kLoop, calls=%fused_computation.10 | loop fusion | flops 10222592 | bytes 5775360 | tf_op jit(solution)/shard_map/reduce_sum | solution.py:80
  472.2 0.7 copy.25
  472.8 0.0 reduce-scatter.5.cloned.1.call-done
  472.8 0.0 reduce-scatter.3.cloned.1.call-done
  472.9 0.0 copy-done.1
  (12 shorter events, 0.1 us)
Async XLA Ops:
  7.2 172.2 %copy-start = (bf16[1,2048,768]{2,1,0:T(8,128)(2,1)S(1)}, bf16[1,2048,768]{2,1,0:T(8,128)(2,1)}, u32[]{:S(2)}) copy-start(bf16[1,2048,768]{2,1,0:T(8,128)(2,1)} %param.10) | copy-start | bytes 9437188
  40.5 11.7 %copy-start.3 = (f32[128,8]{0,1:T(8,128)S(1)}, f32[128,8]{0,1:T(8,128)}, u32[]{:S(2)}) copy-start(f32[128,8]{0,1:T(8,128)} %param.7) | copy-start | bytes 12292
  40.5 130.5 %all-to-all-start = ((bf16[32,40,2048]{2,1,0:T(8,128)(2,1)}), bf16[32,40,2048]{2,1,0:T(8,128)(2,1)}, u32[]{:S(2)}, u32[]{:S(2)}) async-start(bf16[32,40,2048]{2,1,0:T(8,128)(2,1)} %broadcast_select_fusion), calls=%async_computation | async-start | bytes 10485760 | tf_op jit(solution)/shard_map/all_to_all | solution.py:64
  171.0 126.3 %all-to-all-start.2 = ((bf16[32,40,2048]{2,1,0:T(8,128)(2,1)}), bf16[32,40,2048]{2,1,0:T(8,128)(2,1)}, u32[]{:S(2)}, u32[]{:S(2)}) async-start(bf16[32,40,2048]{2,1,0:T(8,128)(2,1)} %fusion), calls=%async_computation.2 | async-start | bytes 10485760 | tf_op jit(solution)/shard_map/all_to_all | solution.py:83
  179.1 293.7 %reduce-scatter.5.cloned.1.call-start = ((), (), s32[]{:S(2)}) async-start(), calls=%async_computation.6 | async-start | bytes 3538944 | tf_op jit(solution)/shard_map/reduce_scatter | solution.py:95
  311.5 161.3 %reduce-scatter.3.cloned.1.call-start = ((), (), s32[]{:S(2)}) async-start(), calls=%async_computation.5 | async-start | bytes 7077888 | tf_op jit(solution)/shard_map/reduce_scatter | solution.py:94
  321.6 1.6 copy-start.4
  327.9 8.3 %copy-start.2 = (bf16[128,2048]{1,0:T(8,128)(2,1)S(1)}, bf16[128,2048]{1,0:T(8,128)(2,1)}, u32[]{:S(2)}) copy-start(bf16[128,2048]{1,0:T(8,128)(2,1)} %param.9) | copy-start | bytes 1572868
  327.9 126.4 %all-to-all-start.1 = ((bf16[32,40,2048]{2,1,0:T(8,128)(2,1)}), bf16[32,40,2048]{2,1,0:T(8,128)(2,1)}, u32[]{:S(2)}, u32[]{:S(2)}) async-start(bf16[32,40,2048]{2,1,0:T(8,128)(2,1)} %bitcast.52), calls=%async_computation.1 | async-start | bytes 10485760 | tf_op jit(solution)/shard_map/all_to_all | solution.py:67
  454.2 18.6 %copy-start.1 = (bf16[1,2048,768]{2,1,0:T(8,128)(2,1)S(1)}, bf16[1,2048,768]{2,1,0:T(8,128)(2,1)}, u32[]{:S(2)}) copy-start(bf16[1,2048,768]{2,1,0:T(8,128)(2,1)} %param.10) | copy-start | bytes 9437188
Sparse Core Ops, SparseCore 0:
  311.6 37.9 reduce-scatter.4
  352.8 44.3 reduce-scatter.2
where the time goes:
time: 480 us
  waiting for transfers between devices  322 us (67%)
  local copies, waits for them, and re-layouts  49.5 us (10%)
  matrix products  37.3 us (8%)
  starting transfers between devices  28.6 us (6%)
  other arithmetic  27.9 us (6%)
  between operations  14.2 us (3%)
    all_to_all x1, waiting for transfers between devices, on_device(): lax.all_to_all(expert_out.reshape(owners, capacity, model_width), 'expert...  117 us
    all_to_all x1, waiting for transfers between devices, on_device(): lax.all_to_all(scaled.reshape(owners, capacity, model_width), 'expert', s...  109 us
    all_to_all x1, waiting for transfers between devices, on_device(): lax.all_to_all(send_rows, 'expert', split_axis=0, concat_axis=0, tiled=True)  95.9 us
    gather x1, local copies, waits for them, and re-layouts, on_device(): returned.reshape(-1, model_width)[target]  12.1 us
    gather x1, local copies, waits for them, and re-layouts, on_device(): cotangent[token_of].astype(jnp.float32)  11.9 us
    gather x1, local copies, waits for them, and re-layouts, on_device(): tokens[token_of]  11.9 us
    all_to_all x1, starting transfers between devices, on_device(): lax.all_to_all(send_rows, 'expert', split_axis=0, concat_axis=0, tiled=True)  11.7 us
    dot_general x1, matrix products, in_gradient(): lax.dot_general(rows_in, grad_pre, (((0,), (0,)), ((), ())), preferred_el...  9.82 us
  transfers between devices with their start and end apart: 5, of which 3 were waited for; matrix products, arithmetic and copies ran while one was open for 14% of the time, Pallas kernels for 0%

commit v1 on v0

v1 whole, which is shorter than its diff:
```python
import jax
import jax.numpy as jnp
from jax import lax
from jax.experimental import pallas as pl
from jax.experimental.pallas import tpu as pltpu
from jax.sharding import Mesh, PartitionSpec as P

BF16 = jnp.bfloat16
F32 = jnp.float32
VMEM_BYTES = 60 * 1024 * 1024
TILE = 256


def params(steps=1):
    return pltpu.CompilerParams(
        dimension_semantics=("arbitrary",) * steps, vmem_limit_bytes=VMEM_BYTES
    )


def cost(flops, moved):
    return pl.CostEstimate(flops=flops, bytes_accessed=moved, transcendentals=0)


def forward_kernel(x_ref, w_ref, silu_ref, slope_ref, hidden_ref):
    rows, width = x_ref.shape
    hidden = hidden_ref.shape[2]
    w = w_ref[...].reshape(width, 2 * hidden)

    @pl.loop(0, rows // TILE)
    def _(i):
        part = pl.ds(pl.multiple_of(i * TILE, TILE), TILE)
        pre = jnp.dot(x_ref[part, :], w, preferred_element_type=F32)
        gate_pre, up_pre = pre[:, :hidden], pre[:, hidden:]
        sig = jax.nn.sigmoid(gate_pre)
        silu = gate_pre * sig
        silu_ref[0, part, :] = silu.astype(BF16)
        slope_ref[0, part, :] = (up_pre * sig * (1.0 + gate_pre * (1.0 - sig))).astype(BF16)
        hidden_ref[0, part, :] = (silu * up_pre).astype(BF16)


def forward(x, w_in_all):
    rows, width = x.shape
    shares, experts, depth, columns = w_in_all.shape
    hidden = columns // 2
    out = jax.ShapeDtypeStruct((experts, rows, hidden), BF16)
    spec = pl.BlockSpec((1, rows, hidden), lambda e: (e, 0, 0))
    return pl.pallas_call(
        forward_kernel,
        grid=(experts,),
        in_specs=[
            pl.BlockSpec((rows, width), lambda e: (0, 0)),
            pl.BlockSpec((shares, 1, depth, columns), lambda e: (0, e, 0, 0)),
        ],
        out_specs=[spec] * 3,
        out_shape=[out] * 3,
        compiler_params=params(),
        cost_estimate=cost(2 * rows * width * columns * experts, 26 << 20),
    )(x, w_in_all)


def hidden_kernel(c_ref, w_ref, g_ref, silu_ref, slope_ref, hidden_ref, pre_ref, hs_ref, hst_ref, gg_ref):
    expert = pl.program_id(0)
    rows, width = c_ref.shape
    hidden = hidden_ref.shape[2]
    w = w_ref[...].reshape(hidden, width)

    @pl.when(expert == 0)
    def _():
        gg_ref[...] = jnp.zeros_like(gg_ref)

    @pl.loop(0, rows // TILE)
    def _(i):
        part = pl.ds(pl.multiple_of(i * TILE, TILE), TILE)
        raw = lax.dot_general(
            c_ref[part, :], w, (((1,), (1,)), ((), ())), preferred_element_type=F32
        )
        lane = lax.broadcasted_iota(jnp.int32, (TILE, g_ref.shape[1]), 1)
        gate = jnp.sum(jnp.where(lane == expert, g_ref[part, :], 0.0), 1, keepdims=True)
        act = hidden_ref[0, part, :].astype(F32)
        inner = jnp.sum(act * raw, 1, keepdims=True)
        gg_ref[part, :] += jnp.where(lane == expert, inner, 0.0)
        scaled = (act * gate).astype(BF16)
        hs_ref[0, part, :] = scaled
        hst_ref[0, :, part] = scaled.T
        grad = raw * gate
        pre_ref[0, part, :hidden] = (grad * slope_ref[0, part, :].astype(F32)).astype(BF16)
        pre_ref[0, part, hidden:] = (grad * silu_ref[0, part, :].astype(F32)).astype(BF16)


def hidden_gradient(c, w_down_all, gates, silu, slope, act):
    rows, width = c.shape
    shares, experts, depth, _ = w_down_all.shape
    hidden = shares * depth
    spec = pl.BlockSpec((1, rows, hidden), lambda e: (e, 0, 0))
    small = pl.BlockSpec((rows, experts), lambda e: (0, 0))
    return pl.pallas_call(
        hidden_kernel,
        grid=(experts,),
        in_specs=[
            pl.BlockSpec((rows, width), lambda e: (0, 0)),
            pl.BlockSpec((shares, 1, depth, width), lambda e: (0, e, 0, 0)),
            small,
            spec,
            spec,
            spec,
        ],
        out_specs=[
            pl.BlockSpec((1, rows, 2 * hidden), lambda e: (e, 0, 0)),
            spec,
            pl.BlockSpec((1, hidden, rows), lambda e: (e, 0, 0)),
            small,
        ],
        out_shape=[
            jax.ShapeDtypeStruct((experts, rows, 2 * hidden), BF16),
            jax.ShapeDtypeStruct((experts, rows, hidden), BF16),
            jax.ShapeDtypeStruct((experts, hidden, rows), BF16),
            jax.ShapeDtypeStruct((rows, experts), F32),
        ],
        compiler_params=params(),
        cost_estimate=cost(2 * rows * width * hidden * experts, 32 << 20),
    )(c, w_down_all, gates, silu, slope, act)


def output_kernel(place_ref, hs_ref, w_ref, out_ref):
    experts, rows, hidden = hs_ref.shape
    width = w_ref.shape[3]
    blocks, block, _ = out_ref.shape
    per_tile = TILE // block

    @pl.loop(0, rows // TILE)
    def _(i):
        part = pl.ds(pl.multiple_of(i * TILE, TILE), TILE)
        total = jnp.zeros((TILE, width), F32)
        for e in range(experts):
            total += jnp.dot(
                hs_ref[e, part, :], w_ref[:, e].reshape(hidden, width), preferred_element_type=F32
            )
        for j in range(per_tile):
            out_ref[pl.ds(place_ref[i * per_tile + j], 1)] = (
                total[j * block : (j + 1) * block].astype(BF16).reshape(1, block, width)
            )


def output_rows(place, hs, w_down_all, block):
    experts, rows, hidden = hs.shape
    shares, _, depth, width = w_down_all.shape
    blocks = rows // block
    columns = 512
    return pl.pallas_call(
        output_kernel,
        grid_spec=pltpu.PrefetchScalarGridSpec(
            num_scalar_prefetch=1,
            grid=(width // columns,),
            in_specs=[
                pl.BlockSpec((experts, rows, hidden), lambda n, p: (0, 0, 0)),
                pl.BlockSpec((shares, experts, depth, columns), lambda n, p: (0, 0, 0, n)),
            ],
            out_specs=pl.BlockSpec((blocks, block, columns), lambda n, p: (0, 0, n)),
        ),
        out_shape=jax.ShapeDtypeStruct((blocks, block, width), BF16),
        compiler_params=params(),
        cost_estimate=cost(2 * rows * width * hidden * experts, 14 << 20),
    )(place, hs, w_down_all)


def weight_kernel(place_ref, x_ref, c_ref, pre_ref, hst_ref, first_ref, second_ref):
    experts, rows, columns = pre_ref.shape
    hidden = hst_ref.shape[1]
    share = x_ref.shape[1]
    half = first_ref.shape[2]
    xt = x_ref[...].T
    c = c_ref[...]

    @pl.loop(0, experts)
    def _(j):
        e = place_ref[j]
        grad_in = jnp.dot(xt, pre_ref[e], preferred_element_type=F32).astype(BF16)
        grad_down = jnp.dot(hst_ref[e], c, preferred_element_type=F32).astype(BF16)
        first_ref[pl.ds(j, 1), 0] = grad_in[:half].reshape(1, half, columns)
        second_ref[0, pl.ds(j, 1), : share - half] = grad_in[half:].reshape(1, share - half, columns)
        piece = hidden // 3
        for i in range(3):
            second_ref[0, pl.ds(j, 1), share - half :, i * share : (i + 1) * share] = grad_down[
                i * piece : (i + 1) * piece
            ].reshape(1, piece, share)


def weight_gradient(place, x, c, pre, hst, ring):
    experts, rows, columns = pre.shape
    hidden = hst.shape[1]
    share = x.shape[1] // (2 * ring)
    half = (share + hidden // 3) // 2
    first = jax.ShapeDtypeStruct((experts, ring, half, columns), BF16)
    second = jax.ShapeDtypeStruct((ring, experts, half, columns), BF16)
    return pl.pallas_call(
        weight_kernel,
        grid_spec=pltpu.PrefetchScalarGridSpec(
            num_scalar_prefetch=1,
            grid=(ring,),
            in_specs=[
                pl.BlockSpec((rows, share), lambda s, p: (0, p[4 + s])),
                pl.BlockSpec((rows, share), lambda s, p: (0, p[4 + s])),
                pl.BlockSpec((experts, rows, columns), lambda s, p: (0, 0, 0)),
                pl.BlockSpec((experts, hidden, rows), lambda s, p: (0, 0, 0)),
            ],
            out_specs=[
                pl.BlockSpec((experts, 1, half, columns), lambda s, p: (0, s, 0, 0)),
                pl.BlockSpec((1, experts, half, columns), lambda s, p: (s, 0, 0, 0)),
            ],
        ),
        out_shape=[first, second],
        compiler_params=params(),
        cost_estimate=cost(rows * x.shape[1] * 3 * hidden * experts, 27 << 20),
    )(place, x, c, pre, hst)


def up(n):
    return [(i, (i + 1) % n) for i in range(n)]


def down(n):
    return [((i + 1) % n, i) for i in range(n)]


def ring_gather(block, axis):
    n = lax.axis_size(axis)
    half = block.shape[0] // 2
    got = {0: block}
    above = below = block
    for step in range(1, n // 2):
        below = lax.ppermute(below, axis, up(n))
        above = lax.ppermute(above, axis, down(n))
        got[step], got[n - step] = below, above
    got[n // 2] = jnp.concatenate(
        [lax.ppermute(below[:half], axis, up(n)), lax.ppermute(above[half:], axis, down(n))], 0
    )
    return jnp.concatenate([got[i] for i in range(n)], 0)


def add(*terms):
    total = terms[0].astype(F32)
    for term in terms[1:]:
        total = total + term.astype(F32)
    return total


def ring_scatter(parts, axis, kind):
    half = parts[0].shape[0] // 2
    low = lax.ppermute(parts[2][:half], axis, up(4))
    high = lax.ppermute(parts[2][half:], axis, down(4))
    to_up = jnp.concatenate([add(parts[1][:half], low).astype(BF16), parts[1][half:]], 0)
    to_down = jnp.concatenate([parts[3][:half], add(parts[3][half:], high).astype(BF16)], 0)
    low = lax.ppermute(to_up, axis, up(4))
    high = lax.ppermute(to_down, axis, down(4))
    return add(parts[0], low, high).astype(kind)


def on_device(tokens, gates, routes, cotangent, w_in, w_down):
    block, width = tokens.shape
    hidden = w_down.shape[1]
    x_at, core_at = lax.axis_index("x"), lax.axis_index("core")
    z_at, y_at = lax.axis_index("z"), lax.axis_index("y")
    z_size, y_size = lax.axis_size("z"), lax.axis_size("y")
    share_at = x_at * 2 + core_at

    small = jnp.concatenate([routes.T.astype(F32), gates.T], 0)
    small = lax.all_gather(small, "z", axis=0)
    order = jnp.remainder(z_at - jnp.arange(z_size), z_size)
    small = small[order]
    top = routes.shape[1]
    ring_routes, ring_gates = small[:, :top].astype(jnp.int32), small[:, top:]
    mine = z_at * y_size + jnp.arange(y_size)
    hit = ring_routes[:, None] == mine[None, :, None, None]
    gate_of = jnp.sum(jnp.where(hit, ring_gates[:, None], 0.0), 2)
    gate_of = jnp.swapaxes(gate_of, 1, 2).reshape(z_size * block, y_size)

    depth_in, depth_down = width // 8, hidden // 8
    share_in = lax.dynamic_slice_in_dim(w_in[0], share_at * depth_in, depth_in, 0)
    share_down = lax.dynamic_slice_in_dim(w_down[0], share_at * depth_down, depth_down, 0)
    w_in_all = lax.all_gather(share_in, ("x", "core", "y"), axis=0, tiled=True)
    w_in_all = w_in_all.reshape(8, y_size, depth_in, 2 * hidden)
    w_down_all = lax.all_gather(share_down, ("x", "core", "y"), axis=0, tiled=True)
    w_down_all = w_down_all.reshape(8, y_size, depth_down, width)

    ring_tokens = ring_gather(tokens, "z")
    ring_cot = ring_gather(cotangent, "z")

    silu, slope, act = forward(ring_tokens, w_in_all)
    pre, hs, hst, gg = hidden_gradient(ring_cot, w_down_all, gate_of, silu, slope, act)

    experts_at = jnp.remainder(y_at + jnp.arange(4), 4)
    shares_at = jnp.remainder(x_at + jnp.arange(4), 4) * 2

    def grads(core):
        place = jnp.concatenate([experts_at, shares_at + core]).astype(jnp.int32)
        return weight_gradient(place, ring_tokens, ring_cot, pre, hst, 4)

    other = grads(1 - core_at)
    swap = [(0, 1), (1, 0)]
    other = [lax.ppermute(g, "core", swap) for g in other]
    partial = output_rows(order.astype(jnp.int32), hs, w_down_all, block)
    mixed_out = lax.psum_scatter(partial, "z", scatter_dimension=0, tiled=True)[0]
    own = grads(core_at)
    first, second = [add(g, h).astype(BF16) for g, h in zip(own, other)]
    first = ring_scatter([first[i] for i in range(4)], "y", BF16)
    second = ring_scatter([second[i] for i in range(4)], "x", BF16)
    first = ring_scatter([first[i] for i in range(4)], "x", F32)
    second = ring_scatter([second[i] for i in range(4)], "y", F32)

    rest = depth_in - first.shape[0]
    grad_in = jnp.concatenate([first, second[:rest]], 0)
    packed = second[rest:]
    grad_down = jnp.concatenate(
        [packed[:, i * depth_in : (i + 1) * depth_in] for i in range(3)], 0
    )

    gg = jnp.swapaxes(gg.reshape(z_size, block, y_size), 1, 2)
    gg = jnp.sum(jnp.where(hit, gg[:, :, None], 0.0), 1)
    grad_gates = lax.psum_scatter(gg[order], "z", scatter_dimension=0, tiled=True)[0].T
    return mixed_out, grad_gates, grad_in[None], grad_down[None]


def solution(mesh):
    wide = Mesh(mesh.devices.reshape(4, 2, 8, 4), ("x", "core", "z", "y"))
    rows = P(("x", "core", "z", "y"), None)
    expert = P(("z", "y"), None, None)
    return jax.shard_map(
        on_device,
        mesh=wide,
        in_specs=(rows, rows, rows, rows, expert, expert),
        out_specs=(
            rows,
            rows,
            P(("z", "y"), ("x", "core"), None),
            P(("z", "y"), None, ("x", "core")),
        ),
        check_vma=False,
    )
```

time: 480 us -> 343 us (0.71)
  waiting for transfers between devices: 322 us -> 40.3 us
  Pallas kernels: 0 us -> 97.2 us
  blocking collectives: 0 us -> 67.6 us
  matrix products: 37.3 us -> 0 us
  starting transfers between devices: 28.6 us -> 63.1 us
  local copies, waits for them, and re-layouts: 49.5 us -> 32.7 us
  other arithmetic: 27.9 us -> 22.8 us
    all_to_all x3 -> x0, waiting for transfers between devices: 322 us -> none  [the longest x1 117 us: on_device(): lax.all_to_all(expert_out.reshape(owners, capacity, model_width), 'expert...]
    pallas_call x0 -> x5, Pallas kernels: none -> 97.2 us  [the longest x2 39.5 us: weight_gradient(): pl.pallas_call(weight_kernel, grid_spec=pltpu.PrefetchScalarGridSpec(num_...]
    ppermute x0 -> x34, starting transfers between devices: none -> 63 us  [the longest x6 14.9 us: ring_gather(): above = lax.ppermute(above, axis, down(n))]
    ppermute x0 -> x34, waiting for transfers between devices: none -> 40.2 us  [the longest x6 22.5 us: ring_gather(): below = lax.ppermute(below, axis, up(n))]
    gather x4 -> x2, local copies, waits for them, and re-layouts: 41 us -> 1.11 us  [the longest x1 0.55 us: on_device(): small = small[order]]
    all_gather x0 -> x1, blocking collectives: none -> 38.1 us  [on_device(): small = lax.all_gather(small, 'z', axis=0)]
    dot_general x5 -> x0, matrix products: 37.3 us -> none  [the longest x1 9.82 us: in_gradient(): lax.dot_general(rows_in, grad_pre, (((0,), (0,)), ((), ())), preferred_el...]
    unnamed x0 -> x1, blocking collectives: none -> 29.5 us
  transfers between devices with their start and end apart: 5 -> 37, of which waited for: 3 -> 11; matrix products, arithmetic and copies ran while one was open for 14% -> 15% of each run, Pallas kernels for 0% -> 17%
where the time goes in v1:
time: 343 us; the launch traced here: 338 us
  Pallas kernels  97.2 us (28%)
  blocking collectives  67.6 us (20%)
  starting transfers between devices  63.1 us (18%)
  waiting for transfers between devices  40.3 us (12%)
  local copies, waits for them, and re-layouts  32.7 us (10%)
  other arithmetic  22.8 us (7%)
  between operations  14.2 us (4%)
    pallas_call x2, Pallas kernels, weight_gradient(): pl.pallas_call(weight_kernel, grid_spec=pltpu.PrefetchScalarGridSpec(num_...  39.5 us
    all_gather x1, blocking collectives, on_device(): small = lax.all_gather(small, 'z', axis=0)  38.1 us
    unnamed x1, blocking collectives  29.5 us
    unnamed x31, local copies, waits for them, and re-layouts  23.5 us
    ppermute x6, waiting for transfers between devices, ring_gather(): below = lax.ppermute(below, axis, up(n))  22.5 us
    pallas_call x1, Pallas kernels, forward(): pl.pallas_call(forward_kernel, grid=(experts,), in_specs=[pl.BlockSpec((r...  22.3 us
    pallas_call x1, Pallas kernels, hidden_gradient(): pl.pallas_call(hidden_kernel, grid=(experts,), in_specs=[pl.BlockSpec((ro...  20 us
    pallas_call x1, Pallas kernels, output_rows(): pl.pallas_call(output_kernel, grid_spec=pltpu.PrefetchScalarGridSpec(num_...  15.3 us
  transfers between devices with their start and end apart: 37, of which 11 were waited for; matrix products, arithmetic and copies ran while one was open for 15% of the time, Pallas kernels for 17%

profile of v1, /device:TPU:24, one launch (start us, length us, event | category | flops | bytes accessed | tf_op | source)
XLA Modules:
  0.0 337.9 jit_solution(18111588991415017052)
XLA Ops:
  7.2 1.8 copy-done
  9.9 1.6 constant_dynamic-slice_fusion.1
  11.6 2.0 collective-permute-start.8
  13.6 4.0 %collective-permute-start.12 = (bf16[128,2048]{1,0:T(8,128)(2,1)}, bf16[128,2048]{1,0:T(8,128)(2,1)S(1)}, u32[]{:S(2)}, u32[]{:S(2)}) collective-permute-start(bf16[128,2048]{1,0:T(8,128)(2,1)} %param.6), channel_id=1, source_target_pairs={{4,0},{8,4},{12,8},{16,12},{20,16},{24,20},{28,24},{0,28},{5,1},{9... | collective-permute-start | bytes 1572872 | tf_op jit(solution)/shard_map/ppermute | solution.py:232
  17.6 3.2 collective-permute-start.4
  22.2 38.1 %all-gather.1 = f32[128,128]{1,0:T(8,128)S(1)} all-gather(f32[16,128]{1,0:T(8,128)S(1)} %pad_maximum_fusion.8), channel_id=3, replica_groups=mesh['x'=4,'core'=2,'z'=8,'y'=4] {'z'}, dimensions={0}, use_global_device_ids=true | all-gather | bytes 73728 | tf_op jit(solution)/shard_map/all_gather | solution.py:267
  61.1 1.9 constant_dynamic-update-slice_fusion.17
  63.0 2.2 collective-permute-start.9
  65.3 1.0 collective-permute-start.13
  66.3 1.0 collective-permute-start.1
  67.3 2.2 collective-permute-start.5
  70.1 1.0 copy.12
  71.2 1.9 constant_dynamic-update-slice_fusion.8
  73.9 5.3 %collective-permute-done.9 = bf16[128,2048]{1,0:T(8,128)(2,1)} collective-permute-done((bf16[128,2048]{1,0:T(8,128)(2,1)S(1)}, bf16[128,2048]{1,0:T(8,128)(2,1)}, u32[]{:S(2)}, u32[]{:S(2)}) %collective-permute-start.9) | collective-permute-done | bytes 524320 | tf_op jit(solution)/shard_map/ppermute | solution.py:231
  79.2 1.0 collective-permute-start.10
  80.2 2.2 collective-permute-start.14
  82.5 8.0 %collective-permute-done.1 = bf16[128,2048]{1,0:T(8,128)(2,1)} collective-permute-done((bf16[128,2048]{1,0:T(8,128)(2,1)S(1)}, bf16[128,2048]{1,0:T(8,128)(2,1)}, u32[]{:S(2)}, u32[]{:S(2)}) %collective-permute-start.1) | collective-permute-done | bytes 524320 | tf_op jit(solution)/shard_map/ppermute | solution.py:231
  90.5 1.0 collective-permute-start.2
  91.5 2.2 collective-permute-start.6
  93.7 1.9 constant_dynamic-update-slice_fusion.7
  95.6 1.9 constant_dynamic-update-slice_fusion.15
  97.5 1.9 constant_dynamic-update-slice_fusion.6
  99.4 2.2 collective-permute-done.10
  101.6 1.1 collective-permute-start.11
  102.7 2.3 collective-permute-start.15
  105.0 7.0 %collective-permute-done.2 = bf16[128,2048]{1,0:T(8,128)(2,1)S(1)} collective-permute-done((bf16[128,2048]{1,0:T(8,128)(2,1)}, bf16[128,2048]{1,0:T(8,128)(2,1)S(1)}, u32[]{:S(2)}, u32[]{:S(2)}) %collective-permute-start.2) | collective-permute-done | bytes 524320 | tf_op jit(solution)/shard_map/ppermute | solution.py:231
  112.1 0.9 collective-permute-start.3
  113.0 2.8 collective-permute-start.7
  116.6 0.9 constant_dynamic-update-slice_fusion.5
  119.0 1.0 collective-permute-done.3
  122.3 1.9 constant_dynamic-update-slice_fusion.10
  125.9 1.9 constant_dynamic-update-slice_fusion.1
  128.6 22.3 %shard_map.93 = (bf16[4,1024,384]{2,1,0:T(8,128)(2,1)}, bf16[4,1024,384]{2,1,0:T(8,128)(2,1)}, bf16[4,1024,384]{2,1,0:T(8,128)(2,1)}) custom-call(bf16[1024,2048]{1,0:T(8,128)(2,1)} %constant_dynamic-update-slice_fusion.9.x_ref, bf16[8,4,256,768]{3,2,1,0:T(8,128)(2,1)} %bitcast.120), custom_call_target="tpu_custom_call" | custom-call | flops 12884901888 | bytes 27262976 | tf_op jit(solution)/shard_map/pallas_call | solution.py:47
  151.0 20.0 %shard_map.94 = (bf16[4,1024,768]{2,1,0:T(8,128)(2,1)}, bf16[4,1024,384]{2,1,0:T(8,128)(2,1)}, bf16[4,384,1024]{2,1,0:T(8,128)(2,1)}, f32[1024,4]{1,0:T(8,128)}) custom-call(bf16[1024,2048]{1,0:T(8,128)(2,1)} %constant_dynamic-update-slice_fusion.c_ref, bf16[8,4,48,2048]{3,2,1,0:T(8,128)(2,1)} %bitcast.121, f32[1024,4]{1,0:T(8,128)} %bitcast.116, ...), custom_call_target="tpu_custom_call" | custom-call | flops 6442450944 | bytes 33554432 | tf_op jit(solution)/shard_map/pallas_call | solution.py:96
  171.0 19.8 %shard_map.97 = (bf16[4,4,192,768]{3,2,1,0:T(8,128)(2,1)}, bf16[4,4,192,768]{3,2,1,0:T(8,128)(2,1)}) custom-call(s32[8]{0:T(128)} %get-tuple-element.56.place_ref, bf16[1024,2048]{1,0:T(8,128)(2,1)} %constant_dynamic-update-slice_fusion.9.x_ref, bf16[1024,2048]{1,0:T(8,128)(2,1)} %constant_dynamic-update-slice_fusion.c_ref, ...), custom_call_target="tpu_custom_call" | custom-call | flops 9663676416 | bytes 28311552 | tf_op jit(solution)/shard_map/pallas_call | solution.py:195
  191.8 15.3 %shard_map.95 = bf16[8,128,2048]{2,1,0:T(8,128)(2,1)} custom-call(s32[8]{0:T(128)} %and_select_fusion.3.place_ref, bf16[4,1024,384]{2,1,0:T(8,128)(2,1)} %get-tuple-element.18.hs_ref, bf16[8,4,48,2048]{3,2,1,0:T(8,128)(2,1)} %bitcast.122), custom_call_target="tpu_custom_call" | custom-call | flops 6442450944 | bytes 14680064 | tf_op jit(solution)/shard_map/pallas_call | solution.py:149
  207.1 19.8 %shard_map.96 = (bf16[4,4,192,768]{3,2,1,0:T(8,128)(2,1)}, bf16[4,4,192,768]{3,2,1,0:T(8,128)(2,1)}) custom-call(s32[8]{0:T(128)} %get-tuple-element.55.place_ref, bf16[1024,2048]{1,0:T(8,128)(2,1)} %constant_dynamic-update-slice_fusion.9.x_ref, bf16[1024,2048]{1,0:T(8,128)(2,1)} %constant_dynamic-update-slice_fusion.c_ref, ...), custom_call_target="tpu_custom_call" | custom-call | flops 9663676416 | bytes 28311552 | tf_op jit(solution)/shard_map/pallas_call | solution.py:195
  226.9 5.3 %add_convert_fusion = bf16[4,4,192,768]{3,2,1,0:T(8,128)(2,1)S(1)} fusion(bf16[4,4,192,768]{3,2,1,0:T(8,128)(2,1)} %collective-permute-done.25, bf16[4,4,192,768]{3,2,1,0:T(8,128)(2,1)} %get-tuple-element.24), kind=kLoop, calls=%fused_computation.2 | loop fusion | flops 9437184 | bytes 14155776 | tf_op jit(solution)/shard_map/convert_element_type | solution.py:304
  232.4 1.7 collective-permute-start.26
  234.1 1.6 collective-permute-start.28
  236.3 3.9 %add_convert_fusion.1 = bf16[4,4,192,768]{3,2,1,0:T(8,128)(2,1)S(1)} fusion(bf16[4,4,192,768]{3,2,1,0:T(8,128)(2,1)} %collective-permute-done.16, bf16[4,4,192,768]{3,2,1,0:T(8,128)(2,1)S(1)} %copy-done.4), kind=kLoop, calls=%fused_computation.3 | loop fusion | flops 9437184 | bytes 14155776 | tf_op jit(solution)/shard_map/convert_element_type | solution.py:304
  240.4 9.4 %collective-permute-start.17 = (bf16[2,192,768]{2,1,0:T(8,128)(2,1)S(1)}, bf16[2,192,768]{2,1,0:T(8,128)(2,1)S(1)}, u32[]{:S(2)}, u32[]{:S(2)}) collective-permute-start(bf16[2,192,768]{2,1,0:T(8,128)(2,1)S(1)} %get-tuple-element.28), channel_id=1, source_target_pairs={{0,1},{1,2},{2,3},{3,0},{4,5},{5,6},{6,7},{7,4},{8,9},{9,10},{10,1... | collective-permute-start | bytes 1769480 | tf_op jit(solution)/shard_map/ppermute | solution.py:249
  249.8 2.0 collective-permute-start.19
  252.2 1.1 pad_maximum_fusion.3
  253.3 2.9 collective-permute-start.29
  256.2 1.1 pad_maximum_fusion.2
  257.3 7.8 %collective-permute-done.17 = bf16[2,192,768]{2,1,0:T(8,128)(2,1)S(1)} collective-permute-done((bf16[2,192,768]{2,1,0:T(8,128)(2,1)S(1)}, bf16[2,192,768]{2,1,0:T(8,128)(2,1)S(1)}, u32[]{:S(2)}, u32[]{:S(2)}) %collective-permute-start.17) | collective-permute-done | bytes 589856 | tf_op jit(solution)/shard_map/ppermute | solution.py:249
  265.1 1.3 collective-permute-done.19
  266.7 1.1 pad_maximum_fusion.1
  268.4 2.9 collective-permute-start.18
  271.8 1.2 copy.13
  273.7 29.5 %all-reduce = f32[8,8,128]{2,1,0:T(8,128)S(1)} all-reduce(f32[8,8,128]{2,1,0:T(8,128)S(1)} %gather_fusion.1), channel_id=6, replica_groups=mesh['x'=4,'core'=2,'z'=8,'y'=4] {'z'}, use_global_device_ids=true, to_apply=%region_3.4.clone | all-reduce | flops 8192 | bytes 65536
  303.2 1.2 dynamic-slice_bitcast_fusion
  304.5 2.4 fusion.1
  307.0 2.0 collective-permute-start.32
  309.1 2.1 fusion.3
  311.2 1.6 collective-permute-start.21
  312.8 1.7 collective-permute-start.23
  315.7 2.9 collective-permute-start.31
  318.7 3.4 %collective-permute-start.24 = (bf16[192,768]{1,0:T(8,128)(2,1)S(1)}, bf16[192,768]{1,0:T(8,128)(2,1)S(1)}, u32[]{:S(2)}, u32[]{:S(2)}) collective-permute-start(bf16[192,768]{1,0:T(8,128)(2,1)S(1)} %pad_maximum_fusion.5), channel_id=1, source_target_pairs={{64,0},{128,64},{192,128},{0,192},{65,1},{129,65},{193,129},{1,193... | collective-permute-start | bytes 884744 | tf_op jit(solution)/shard_map/ppermute | solution.py:254
  322.2 0.9 collective-permute-done.33
  324.1 2.2 collective-permute-done.24
  326.3 3.8 %collective-permute-done.22 = bf16[192,768]{1,0:T(8,128)(2,1)S(1)} collective-permute-done((bf16[192,768]{1,0:T(8,128)(2,1)S(1)}, bf16[192,768]{1,0:T(8,128)(2,1)S(1)}, u32[]{:S(2)}, u32[]{:S(2)}) %collective-permute-start.22) | collective-permute-done | bytes 294944 | tf_op jit(solution)/shard_map/ppermute | solution.py:253
  330.2 0.9 maximum_bitcast_fusion
  (102 shorter events, 18.8 us)
Async XLA Ops:
  7.2 1.9 copy-start
  7.2 121.5 %all-gather.8.cloned.1.call-start = ((), (), s32[]{:S(2)}) async-start(), calls=%async_computation.3 | async-start | bytes 12976128 | tf_op jit(solution)/shard_map/all_gather | solution.py:280
  9.9 141.1 %all-gather.6.cloned.1.call-start = ((), (), s32[]{:S(2)}) async-start(), calls=%async_computation.2 | async-start | bytes 6488064 | tf_op jit(solution)/shard_map/all_gather | solution.py:282
  11.6 319.6 %reduce-scatter.2.cloned.1.call-start = ((), (), s32[]{:S(2)}) async-start(), calls=%async_computation.1 | async-start | bytes 4718592 | tf_op jit(solution)/shard_map/reduce_scatter | solution.py:302
  11.6 51.4 %collective-permute-start.8 = (bf16[128,2048]{1,0:T(8,128)(2,1)}, bf16[128,2048]{1,0:T(8,128)(2,1)S(1)}, u32[]{:S(2)}, u32[]{:S(2)}) collective-permute-start(bf16[128,2048]{1,0:T(8,128)(2,1)} %param.6), channel_id=1, source_target_pairs={{0,4},{4,8},{8,12},{12,16},{16,20},{20,24},{24,28},{28,0},{1,5},{5... | collective-permute-start | bytes 1572872 | tf_op jit(solution)/shard_map/ppermute | solution.py:231
  13.6 51.7 %collective-permute-start.12 = (bf16[128,2048]{1,0:T(8,128)(2,1)}, bf16[128,2048]{1,0:T(8,128)(2,1)S(1)}, u32[]{:S(2)}, u32[]{:S(2)}) collective-permute-start(bf16[128,2048]{1,0:T(8,128)(2,1)} %param.6), channel_id=1, source_target_pairs={{4,0},{8,4},{12,8},{16,12},{20,16},{24,20},{28,24},{0,28},{5,1},{9... | collective-permute-start | bytes 1572872 | tf_op jit(solution)/shard_map/ppermute | solution.py:232
  17.6 48.7 %collective-permute-start = (bf16[128,2048]{1,0:T(8,128)(2,1)}, bf16[128,2048]{1,0:T(8,128)(2,1)S(1)}, u32[]{:S(2)}, u32[]{:S(2)}) collective-permute-start(bf16[128,2048]{1,0:T(8,128)(2,1)} %param.9), channel_id=1, source_target_pairs={{0,4},{4,8},{8,12},{12,16},{16,20},{20,24},{24,28},{28,0},{1,5},{5... | collective-permute-start | bytes 1572872 | tf_op jit(solution)/shard_map/ppermute | solution.py:231
  17.6 49.7 %collective-permute-start.4 = (bf16[128,2048]{1,0:T(8,128)(2,1)}, bf16[128,2048]{1,0:T(8,128)(2,1)S(1)}, u32[]{:S(2)}, u32[]{:S(2)}) collective-permute-start(bf16[128,2048]{1,0:T(8,128)(2,1)} %param.9), channel_id=1, source_target_pairs={{4,0},{8,4},{12,8},{16,12},{20,16},{24,20},{28,24},{0,28},{5,1},{9... | collective-permute-start | bytes 1572872 | tf_op jit(solution)/shard_map/ppermute | solution.py:232
  63.0 16.2 %collective-permute-start.9 = (bf16[128,2048]{1,0:T(8,128)(2,1)S(1)}, bf16[128,2048]{1,0:T(8,128)(2,1)}, u32[]{:S(2)}, u32[]{:S(2)}) collective-permute-start(bf16[128,2048]{1,0:T(8,128)(2,1)S(1)} %collective-permute-done.8), channel_id=1, source_target_pairs={{0,4},{4,8},{8,12},{12,16},{16,20},{20,24},{24,28},{28,0},{1,5},{5... | collective-permute-start | bytes 1572872 | tf_op jit(solution)/shard_map/ppermute | solution.py:231
  65.3 15.0 %collective-permute-start.13 = (bf16[128,2048]{1,0:T(8,128)(2,1)S(1)}, bf16[128,2048]{1,0:T(8,128)(2,1)}, u32[]{:S(2)}, u32[]{:S(2)}) collective-permute-start(bf16[128,2048]{1,0:T(8,128)(2,1)S(1)} %collective-permute-done.12), channel_id=1, source_target_pairs={{4,0},{8,4},{12,8},{16,12},{20,16},{24,20},{28,24},{0,28},{5,1},{9... | collective-permute-start | bytes 1572872 | tf_op jit(solution)/shard_map/ppermute | solution.py:232
  66.3 25.2 %copy-start.5 = (bf16[128,2048]{1,0:T(8,128)(2,1)}, bf16[128,2048]{1,0:T(8,128)(2,1)S(1)}, u32[]{:S(2)}) copy-start(bf16[128,2048]{1,0:T(8,128)(2,1)S(1)} %collective-permute-done) | copy-start | bytes 1572868
  66.3 24.2 %collective-permute-start.1 = (bf16[128,2048]{1,0:T(8,128)(2,1)S(1)}, bf16[128,2048]{1,0:T(8,128)(2,1)}, u32[]{:S(2)}, u32[]{:S(2)}) collective-permute-start(bf16[128,2048]{1,0:T(8,128)(2,1)S(1)} %collective-permute-done), channel_id=1, source_target_pairs={{0,4},{4,8},{8,12},{12,16},{16,20},{20,24},{24,28},{28,0},{1,5},{5... | collective-permute-start | bytes 1572872 | tf_op jit(solution)/shard_map/ppermute | solution.py:231
  67.3 24.2 %collective-permute-start.5 = (bf16[128,2048]{1,0:T(8,128)(2,1)S(1)}, bf16[128,2048]{1,0:T(8,128)(2,1)}, u32[]{:S(2)}, u32[]{:S(2)}) collective-permute-start(bf16[128,2048]{1,0:T(8,128)(2,1)S(1)} %collective-permute-done.4), channel_id=1, source_target_pairs={{4,0},{8,4},{12,8},{16,12},{20,16},{24,20},{28,24},{0,28},{5,1},{9... | collective-permute-start | bytes 1572872 | tf_op jit(solution)/shard_map/ppermute | solution.py:232
  79.2 22.4 %collective-permute-start.10 = (bf16[128,2048]{1,0:T(8,128)(2,1)}, bf16[128,2048]{1,0:T(8,128)(2,1)S(1)}, u32[]{:S(2)}, u32[]{:S(2)}) collective-permute-start(bf16[128,2048]{1,0:T(8,128)(2,1)} %collective-permute-done.9), channel_id=1, source_target_pairs={{0,4},{4,8},{8,12},{12,16},{16,20},{20,24},{24,28},{28,0},{1,5},{5... | collective-permute-start | bytes 1572872 | tf_op jit(solution)/shard_map/ppermute | solution.py:231
  80.2 22.5 %collective-permute-start.14 = (bf16[128,2048]{1,0:T(8,128)(2,1)}, bf16[128,2048]{1,0:T(8,128)(2,1)S(1)}, u32[]{:S(2)}, u32[]{:S(2)}) collective-permute-start(bf16[128,2048]{1,0:T(8,128)(2,1)} %collective-permute-done.13), channel_id=1, source_target_pairs={{4,0},{8,4},{12,8},{16,12},{20,16},{24,20},{28,24},{0,28},{5,1},{9... | collective-permute-start | bytes 1572872 | tf_op jit(solution)/shard_map/ppermute | solution.py:232
  90.5 21.6 %collective-permute-start.2 = (bf16[128,2048]{1,0:T(8,128)(2,1)}, bf16[128,2048]{1,0:T(8,128)(2,1)S(1)}, u32[]{:S(2)}, u32[]{:S(2)}) collective-permute-start(bf16[128,2048]{1,0:T(8,128)(2,1)} %collective-permute-done.1), channel_id=1, source_target_pairs={{0,4},{4,8},{8,12},{12,16},{16,20},{20,24},{24,28},{28,0},{1,5},{5... | collective-permute-start | bytes 1572872 | tf_op jit(solution)/shard_map/ppermute | solution.py:231
  91.5 21.5 %collective-permute-start.6 = (bf16[128,2048]{1,0:T(8,128)(2,1)}, bf16[128,2048]{1,0:T(8,128)(2,1)S(1)}, u32[]{:S(2)}, u32[]{:S(2)}) collective-permute-start(bf16[128,2048]{1,0:T(8,128)(2,1)} %collective-permute-done.5), channel_id=1, source_target_pairs={{4,0},{8,4},{12,8},{16,12},{20,16},{24,20},{28,24},{0,28},{5,1},{9... | collective-permute-start | bytes 1572872 | tf_op jit(solution)/shard_map/ppermute | solution.py:232
  101.6 15.9 %collective-permute-start.11 = (bf16[64,2048]{1,0:T(8,128)(2,1)S(1)}, bf16[64,2048]{1,0:T(8,128)(2,1)S(1)}, u32[]{:S(2)}, u32[]{:S(2)}) collective-permute-start(bf16[64,2048]{1,0:T(8,128)(2,1)S(1)} %slice.272), channel_id=1, source_target_pairs={{0,4},{4,8},{8,12},{12,16},{16,20},{20,24},{24,28},{28,0},{1,5},{5... | collective-permute-start | bytes 786440 | tf_op jit(solution)/shard_map/ppermute | solution.py:235
  102.7 15.5 %collective-permute-start.15 = (bf16[64,2048]{1,0:T(8,128)(2,1)S(1)}, bf16[64,2048]{1,0:T(8,128)(2,1)S(1)}, u32[]{:S(2)}, u32[]{:S(2)}) collective-permute-start(bf16[64,2048]{1,0:T(8,128)(2,1)S(1)} %slice.273), channel_id=1, source_target_pairs={{4,0},{8,4},{12,8},{16,12},{20,16},{24,20},{28,24},{0,28},{5,1},{9... | collective-permute-start | bytes 786440 | tf_op jit(solution)/shard_map/ppermute | solution.py:235
  112.1 7.9 %collective-permute-start.3 = (bf16[64,2048]{1,0:T(8,128)(2,1)S(1)}, bf16[64,2048]{1,0:T(8,128)(2,1)S(1)}, u32[]{:S(2)}, u32[]{:S(2)}) collective-permute-start(bf16[64,2048]{1,0:T(8,128)(2,1)S(1)} %slice.268), channel_id=1, source_target_pairs={{0,4},{4,8},{8,12},{12,16},{16,20},{20,24},{24,28},{28,0},{1,5},{5... | collective-permute-start | bytes 786440 | tf_op jit(solution)/shard_map/ppermute | solution.py:235
  113.0 7.8 %collective-permute-start.7 = (bf16[64,2048]{1,0:T(8,128)(2,1)S(1)}, bf16[64,2048]{1,0:T(8,128)(2,1)S(1)}, u32[]{:S(2)}, u32[]{:S(2)}) collective-permute-start(bf16[64,2048]{1,0:T(8,128)(2,1)S(1)} %slice.269), channel_id=1, source_target_pairs={{4,0},{8,4},{12,8},{16,12},{20,16},{24,20},{28,24},{0,28},{5,1},{9... | collective-permute-start | bytes 786440 | tf_op jit(solution)/shard_map/ppermute | solution.py:235
  190.7 36.2 %collective-permute-start.25 = (bf16[4,4,192,768]{3,2,1,0:T(8,128)(2,1)}, bf16[4,4,192,768]{3,2,1,0:T(8,128)(2,1)}, u32[]{:S(2)}, u32[]{:S(2)}) collective-permute-start(bf16[4,4,192,768]{3,2,1,0:T(8,128)(2,1)} %get-tuple-element.25), channel_id=1, source_target_pairs={{0,32},{32,0},{1,33},{33,1},{2,34},{34,2},{3,35},{35,3},{4,36},{36... | collective-permute-start | bytes 14155784 | tf_op jit(solution)/shard_map/ppermute | solution.py:300
  190.8 45.0 %collective-permute-start.16 = (bf16[4,4,192,768]{3,2,1,0:T(8,128)(2,1)}, bf16[4,4,192,768]{3,2,1,0:T(8,128)(2,1)}, u32[]{:S(2)}, u32[]{:S(2)}) collective-permute-start(bf16[4,4,192,768]{3,2,1,0:T(8,128)(2,1)} %get-tuple-element.23), channel_id=1, source_target_pairs={{0,32},{32,0},{1,33},{33,1},{2,34},{34,2},{3,35},{35,3},{4,36},{36... | collective-permute-start | bytes 14155784 | tf_op jit(solution)/shard_map/ppermute | solution.py:300
  232.2 19.6 %copy-start.3 = (bf16[4,4,192,768]{3,2,1,0:T(8,128)(2,1)}, bf16[4,4,192,768]{3,2,1,0:T(8,128)(2,1)S(1)}, u32[]{:S(2)}) copy-start(bf16[4,4,192,768]{3,2,1,0:T(8,128)(2,1)S(1)} %add_convert_fusion) | copy-start | bytes 14155780
  232.2 4.1 %copy-start.4 = (bf16[4,4,192,768]{3,2,1,0:T(8,128)(2,1)S(1)}, bf16[4,4,192,768]{3,2,1,0:T(8,128)(2,1)}, u32[]{:S(2)}) copy-start(bf16[4,4,192,768]{3,2,1,0:T(8,128)(2,1)} %get-tuple-element.22) | copy-start | bytes 14155780
  232.4 19.4 %collective-permute-start.26 = (bf16[2,192,768]{2,1,0:T(8,128)(2,1)S(1)}, bf16[2,192,768]{2,1,0:T(8,128)(2,1)S(1)}, u32[]{:S(2)}, u32[]{:S(2)}) collective-permute-start(bf16[2,192,768]{2,1,0:T(8,128)(2,1)S(1)} %get-tuple-element.34), channel_id=1, source_target_pairs={{0,64},{64,128},{128,192},{192,0},{1,65},{65,129},{129,193},{193,1... | collective-permute-start | bytes 1769480 | tf_op jit(solution)/shard_map/ppermute | solution.py:249
  234.1 17.7 %collective-permute-start.28 = (bf16[2,192,768]{2,1,0:T(8,128)(2,1)S(1)}, bf16[2,192,768]{2,1,0:T(8,128)(2,1)S(1)}, u32[]{:S(2)}, u32[]{:S(2)}) collective-permute-start(bf16[2,192,768]{2,1,0:T(8,128)(2,1)S(1)} %get-tuple-element.35), channel_id=1, source_target_pairs={{64,0},{128,64},{192,128},{0,192},{65,1},{129,65},{193,129},{1,193... | collective-permute-start | bytes 1769480 | tf_op jit(solution)/shard_map/ppermute | solution.py:250
  240.2 26.1 %copy-start.2 = (bf16[4,4,192,768]{3,2,1,0:T(8,128)(2,1)}, bf16[4,4,192,768]{3,2,1,0:T(8,128)(2,1)S(1)}, u32[]{:S(2)}) copy-start(bf16[4,4,192,768]{3,2,1,0:T(8,128)(2,1)S(1)} %add_convert_fusion.1) | copy-start | bytes 14155780
  240.4 24.7 %collective-permute-start.17 = (bf16[2,192,768]{2,1,0:T(8,128)(2,1)S(1)}, bf16[2,192,768]{2,1,0:T(8,128)(2,1)S(1)}, u32[]{:S(2)}, u32[]{:S(2)}) collective-permute-start(bf16[2,192,768]{2,1,0:T(8,128)(2,1)S(1)} %get-tuple-element.28), channel_id=1, source_target_pairs={{0,1},{1,2},{2,3},{3,0},{4,5},{5,6},{6,7},{7,4},{8,9},{9,10},{10,1... | collective-permute-start | bytes 1769480 | tf_op jit(solution)/shard_map/ppermute | solution.py:249
  249.8 16.6 %collective-permute-start.19 = (bf16[2,192,768]{2,1,0:T(8,128)(2,1)S(1)}, bf16[2,192,768]{2,1,0:T(8,128)(2,1)S(1)}, u32[]{:S(2)}, u32[]{:S(2)}) collective-permute-start(bf16[2,192,768]{2,1,0:T(8,128)(2,1)S(1)} %get-tuple-element.29), channel_id=1, source_target_pairs={{1,0},{2,1},{3,2},{0,3},{5,4},{6,5},{7,6},{4,7},{9,8},{10,9},{11,1... | collective-permute-start | bytes 1769480 | tf_op jit(solution)/shard_map/ppermute | solution.py:250
  253.3 51.2 %collective-permute-start.29 = (bf16[4,192,768]{2,1,0:T(8,128)(2,1)}, bf16[4,192,768]{2,1,0:T(8,128)(2,1)}, u32[]{:S(2)}, u32[]{:S(2)}) collective-permute-start(bf16[4,192,768]{2,1,0:T(8,128)(2,1)} %pad_maximum_fusion.3), channel_id=1, source_target_pairs={{64,0},{128,64},{192,128},{0,192},{65,1},{129,65},{193,129},{1,193... | collective-permute-start | bytes 3538952 | tf_op jit(solution)/shard_map/ppermute | solution.py:254
  257.3 13.9 %copy-start.6 = (u32[256]{0:T(256)S(1)}, u32[256]{0:T(256)}, u32[]{:S(2)}) copy-start(u32[256]{0:T(256)} %constant.83) | copy-start | bytes 3076
  257.3 47.2 %collective-permute-start.27 = (bf16[4,192,768]{2,1,0:T(8,128)(2,1)}, bf16[4,192,768]{2,1,0:T(8,128)(2,1)}, u32[]{:S(2)}, u32[]{:S(2)}) collective-permute-start(bf16[4,192,768]{2,1,0:T(8,128)(2,1)} %pad_maximum_fusion.2), channel_id=1, source_target_pairs={{0,64},{64,128},{128,192},{192,0},{1,65},{65,129},{129,193},{193,1... | collective-permute-start | bytes 3538952 | tf_op jit(solution)/shard_map/ppermute | solution.py:253
  267.8 41.2 %collective-permute-start.20 = (bf16[4,192,768]{2,1,0:T(8,128)(2,1)}, bf16[4,192,768]{2,1,0:T(8,128)(2,1)}, u32[]{:S(2)}, u32[]{:S(2)}) collective-permute-start(bf16[4,192,768]{2,1,0:T(8,128)(2,1)} %pad_maximum_fusion.1), channel_id=1, source_target_pairs={{1,0},{2,1},{3,2},{0,3},{5,4},{6,5},{7,6},{4,7},{9,8},{10,9},{11,1... | collective-permute-start | bytes 3538952 | tf_op jit(solution)/shard_map/ppermute | solution.py:254
  268.4 40.7 %collective-permute-start.18 = (bf16[4,192,768]{2,1,0:T(8,128)(2,1)S(1)}, bf16[4,192,768]{2,1,0:T(8,128)(2,1)S(1)}, u32[]{:S(2)}, u32[]{:S(2)}) collective-permute-start(bf16[4,192,768]{2,1,0:T(8,128)(2,1)S(1)} %pad_maximum_fusion), channel_id=1, source_target_pairs={{0,1},{1,2},{2,3},{3,0},{4,5},{5,6},{6,7},{7,4},{8,9},{9,10},{10,1... | collective-permute-start | bytes 3538952 | tf_op jit(solution)/shard_map/ppermute | solution.py:253
  306.9 7.5 %collective-permute-start.30 = (bf16[96,768]{1,0:T(8,128)(2,1)S(1)}, bf16[96,768]{1,0:T(8,128)(2,1)S(1)}, u32[]{:S(2)}, u32[]{:S(2)}) collective-permute-start(bf16[96,768]{1,0:T(8,128)(2,1)S(1)} %get-tuple-element.46), channel_id=1, source_target_pairs={{0,1},{1,2},{2,3},{3,0},{4,5},{5,6},{6,7},{7,4},{8,9},{9,10},{10,1... | collective-permute-start | bytes 442376 | tf_op jit(solution)/shard_map/ppermute | solution.py:249
  307.0 8.0 %collective-permute-start.32 = (bf16[96,768]{1,0:T(8,128)(2,1)S(1)}, bf16[96,768]{1,0:T(8,128)(2,1)S(1)}, u32[]{:S(2)}, u32[]{:S(2)}) collective-permute-start(bf16[96,768]{1,0:T(8,128)(2,1)S(1)} %get-tuple-element.47), channel_id=1, source_target_pairs={{1,0},{2,1},{3,2},{0,3},{5,4},{6,5},{7,6},{4,7},{9,8},{10,9},{11,1... | collective-permute-start | bytes 442376 | tf_op jit(solution)/shard_map/ppermute | solution.py:250
  311.2 7.4 %collective-permute-start.21 = (bf16[96,768]{1,0:T(8,128)(2,1)S(1)}, bf16[96,768]{1,0:T(8,128)(2,1)S(1)}, u32[]{:S(2)}, u32[]{:S(2)}) collective-permute-start(bf16[96,768]{1,0:T(8,128)(2,1)S(1)} %get-tuple-element.40), channel_id=1, source_target_pairs={{0,64},{64,128},{128,192},{192,0},{1,65},{65,129},{129,193},{193,1... | collective-permute-start | bytes 442376 | tf_op jit(solution)/shard_map/ppermute | solution.py:249
  312.8 5.8 %collective-permute-start.23 = (bf16[96,768]{1,0:T(8,128)(2,1)S(1)}, bf16[96,768]{1,0:T(8,128)(2,1)S(1)}, u32[]{:S(2)}, u32[]{:S(2)}) collective-permute-start(bf16[96,768]{1,0:T(8,128)(2,1)S(1)} %get-tuple-element.41), channel_id=1, source_target_pairs={{64,0},{128,64},{192,128},{0,192},{65,1},{129,65},{193,129},{1,193... | collective-permute-start | bytes 442376 | tf_op jit(solution)/shard_map/ppermute | solution.py:250
  315.1 8.0 %collective-permute-start.33 = (bf16[192,768]{1,0:T(8,128)(2,1)S(1)}, bf16[192,768]{1,0:T(8,128)(2,1)S(1)}, u32[]{:S(2)}, u32[]{:S(2)}) collective-permute-start(bf16[192,768]{1,0:T(8,128)(2,1)S(1)} %pad_maximum_fusion.7), channel_id=1, source_target_pairs={{1,0},{2,1},{3,2},{0,3},{5,4},{6,5},{7,6},{4,7},{9,8},{10,9},{11,1... | collective-permute-start | bytes 884744 | tf_op jit(solution)/shard_map/ppermute | solution.py:254
  315.7 15.5 %copy-start.1 = (bf16[1,2048,768]{2,1,0:T(8,128)(2,1)S(1)}, bf16[1,2048,768]{2,1,0:T(8,128)(2,1)}, u32[]{:S(2)}) copy-start(bf16[1,2048,768]{2,1,0:T(8,128)(2,1)} %param.10) | copy-start | bytes 9437188
  315.7 7.4 %collective-permute-start.31 = (bf16[192,768]{1,0:T(8,128)(2,1)S(1)}, bf16[192,768]{1,0:T(8,128)(2,1)S(1)}, u32[]{:S(2)}, u32[]{:S(2)}) collective-permute-start(bf16[192,768]{1,0:T(8,128)(2,1)S(1)} %pad_maximum_fusion.6), channel_id=1, source_target_pairs={{0,1},{1,2},{2,3},{3,0},{4,5},{5,6},{6,7},{7,4},{8,9},{9,10},{10,1... | collective-permute-start | bytes 884744 | tf_op jit(solution)/shard_map/ppermute | solution.py:253
  318.7 7.7 %collective-permute-start.24 = (bf16[192,768]{1,0:T(8,128)(2,1)S(1)}, bf16[192,768]{1,0:T(8,128)(2,1)S(1)}, u32[]{:S(2)}, u32[]{:S(2)}) collective-permute-start(bf16[192,768]{1,0:T(8,128)(2,1)S(1)} %pad_maximum_fusion.5), channel_id=1, source_target_pairs={{64,0},{128,64},{192,128},{0,192},{65,1},{129,65},{193,129},{1,193... | collective-permute-start | bytes 884744 | tf_op jit(solution)/shard_map/ppermute | solution.py:254
  322.1 8.0 %collective-permute-start.22 = (bf16[192,768]{1,0:T(8,128)(2,1)S(1)}, bf16[192,768]{1,0:T(8,128)(2,1)S(1)}, u32[]{:S(2)}, u32[]{:S(2)}) collective-permute-start(bf16[192,768]{1,0:T(8,128)(2,1)S(1)} %pad_maximum_fusion.4), channel_id=1, source_target_pairs={{0,64},{64,128},{128,192},{192,0},{1,65},{65,129},{129,193},{193,1... | collective-permute-start | bytes 884744 | tf_op jit(solution)/shard_map/ppermute | solution.py:253
Sparse Core Ops, SparseCore 0:
  11.2 70.1 all-gather.7
  84.0 53.2 all-gather.5
  207.3 54.3 reduce-scatter.1
